TPU v7x, 32 devices: a whole 2x2x4 slice. The times are simulated.
32 devices in a mesh: groups: 2 (over y), uv: 4 (over z), chan: 2 (over x), pol: 2 (over core).
Axes of the slice: x: 2, y: 2, z: 4, core: 2. Of those that a mesh axis runs over, the one named last changes fastest.
Arguments:
- visibilities: bfloat16 [8, 256, 2, 128], P(('groups', 'chan', 'pol'), 'uv'), parts along dimension 0, may hold values from -6 to 6
- tile_pairs: int32 [512, 2, 128], P(('groups', 'uv')), parts along dimension 0, may hold values from 0 to 255
- owner_tiles: int32 [8, 256, 1], P(('groups', 'chan', 'pol'), 'uv'), parts along dimension 0, may hold values from 0 to 3; in each aligned block of 64 rows (0 to 63, 64 to 127, ..., all dimensions but the last counted through in order) at most 32 rows name the same one
- cell_ids: int32 [8, 256], P(('groups', 'chan', 'pol'), 'uv'), parts along dimension 0, may hold values from 0 to 255
- gains: float32 [8, 2, 256], P(('groups', 'chan', 'pol')), parts along dimension 0, may hold values from -4 to 4
- beams: float32 [256, 128], replicated, may hold values from -6 to 6
- support: int32 [256, 8], replicated, may hold values 0 or 1
Outputs:
- image: float32 [8, 2, 2048, 2048], P(('groups', 'chan', 'pol'), None, 'uv'), parts along dimension 0
There are 2 independent parts, one for each index of `groups`. A program takes and returns all parts, laid end to end along the dimension named above; an argument that names none is the same for every part. Nothing has to cross between parts.
Inputs may be any that keep to these rules, and one draw needn't show every extreme that they name: `owner_tiles`: in each plane, the 64 blocks of one device along uv name no uv tile more than 32 times, a bound that some block reaches.
All inputs are finite; a program needn't handle non-finite values.
Results may differ from a plain program's by a relative error of at most 0.0052.
Values may be sent and summed in bfloat16 or wider, within the bound.
A program may use at most 128 MiB of HBM per device.

v0:
```python
import math

import jax
import jax.numpy as jnp
from jax import lax
from jax.sharding import PartitionSpec as P

GRID = 2048


def kernel_table(beams, support):
    half_width = beams.shape[1] // 2
    band_width = half_width // 4
    mask_along_u = jnp.repeat(support[:, :4], band_width, axis=1)
    mask_along_v = jnp.repeat(support[:, 4:], band_width, axis=1)
    return beams * jnp.concatenate([mask_along_u, mask_along_v], axis=1).astype(jnp.float32)


def table_lookup(lookup_table, indices):
    selector_matrix = (
        indices[..., None] == jnp.arange(lookup_table.shape[0], dtype=jnp.int32)
    ).astype(jnp.float32)
    return jnp.einsum("ijm,mv->ijv", selector_matrix, lookup_table, precision=lax.Precision.HIGHEST)


def gain_and_grid(raw_part, first_tile, second_tile, joint_table):
    half_width = (joint_table.shape[1] - 2) // 2
    first_rows = table_lookup(joint_table, first_tile)
    second_rows = table_lookup(joint_table, second_tile)
    leading_real = first_rows[..., 2 * half_width]
    first_imag = first_rows[..., 2 * half_width + 1]
    second_real = second_rows[..., 2 * half_width]
    second_imag = second_rows[..., 2 * half_width + 1]
    visibility_real = raw_part[:, 0, :].astype(jnp.float32)
    vis_imag = raw_part[:, 1, :].astype(jnp.float32)
    prod_real = leading_real * visibility_real - first_imag * vis_imag
    prod_imag = leading_real * vis_imag + first_imag * visibility_real
    gained_real = prod_real * second_real + prod_imag * second_imag
    gained_imag = prod_imag * second_real - prod_real * second_imag
    convolution_kernels = first_rows[..., : 2 * half_width] * second_rows[..., : 2 * half_width]
    along_u = convolution_kernels[..., :half_width]
    along_v = convolution_kernels[..., half_width:]
    weighted = jnp.concatenate(
        [gained_real[..., None] * along_v, gained_imag[..., None] * along_v], axis=-1
    )
    return jnp.einsum("gra,grx->gax", along_u, weighted, precision=lax.Precision.HIGHEST)


def dft_tables(offset, block_width, total):
    row_index = offset + jnp.arange(block_width, dtype=jnp.int32)
    col_index = jnp.arange(total, dtype=jnp.int32)
    products = row_index[:, None] * col_index[None, :] % total
    angles = products.astype(jnp.float32) * (2.0 * math.pi / total)
    return (jnp.cos(angles).astype(jnp.bfloat16), jnp.sin(angles).astype(jnp.bfloat16))


def place_cells(cell_part, sub_grids, cell_count):
    deposited_cells = (
        cell_part[:, None] == jnp.arange(cell_count, dtype=jnp.int32)[None, :]
    ).astype(jnp.float32)
    return jnp.einsum("sc,sax->cax", deposited_cells, sub_grids, precision=lax.Precision.HIGHEST)


def on_device(visibilities, tile_pairs, owner_tiles, cell_ids, gains, beams, support):
    owner_count = lax.axis_size("uv")
    raw_blocks = visibilities[0]
    nblocks = raw_blocks.shape[0]
    rows_each = raw_blocks.shape[2]
    capacity = 2 * nblocks // owner_count
    slot_count = owner_count * capacity
    kernel_size = beams.shape[1] // 2
    grid_size = GRID
    strip_rows = grid_size // owner_count
    columns = grid_size // kernel_size
    band_count = strip_rows // kernel_size
    cell_count = band_count * columns
    beam_table = kernel_table(beams, support)
    owner_ids = owner_tiles[0, :, 0]
    cell_list = cell_ids[0]
    plane_gains = gains[0]
    joint_table = jnp.concatenate([beam_table, plane_gains.T], axis=1)
    chosen = (owner_ids[:, None] == jnp.arange(owner_count, dtype=jnp.int32)[None, :]).astype(
        jnp.int32
    )
    position = jnp.sum((jnp.cumsum(chosen, axis=0) - 1) * chosen, axis=1)
    target = owner_ids * capacity + position
    matches = (target[None, :] == jnp.arange(slot_count, dtype=jnp.int32)[:, None]).astype(
        jnp.int32
    )
    match_float = matches.astype(jnp.float32)
    slot_cells = jnp.sum(matches * cell_list[None, :], axis=1)
    group_size = 8

    def grid_group(pieces):
        return gain_and_grid(pieces[0], pieces[1], pieces[2], joint_table)

    stacked = (
        raw_blocks.reshape(nblocks // group_size, group_size, 2, rows_each),
        tile_pairs[:, 0, :].reshape(nblocks // group_size, group_size, rows_each),
        tile_pairs[:, 1, :].reshape(nblocks // group_size, group_size, rows_each),
    )
    subgrids = lax.map(grid_group, stacked).reshape(nblocks, kernel_size * 2 * kernel_size)
    outgoing = jnp.dot(
        match_float, subgrids, precision=lax.Precision.HIGHEST, preferred_element_type=jnp.float32
    ).reshape(slot_count, kernel_size, 2 * kernel_size)
    received, got_cell = (
        lax.all_to_all(outgoing, "uv", split_axis=0, concat_axis=0, tiled=True),
        lax.all_to_all(slot_cells, "uv", split_axis=0, concat_axis=0, tiled=True),
    )
    strip_sum = place_cells(got_cell, received, cell_count)
    uv_plane = strip_sum.reshape(band_count, columns, kernel_size, 2, kernel_size).transpose(
        3, 0, 2, 1, 4
    )
    uv_plane = uv_plane.reshape(2 * strip_rows, grid_size).astype(jnp.bfloat16)
    block_width = min(512, grid_size)
    scale_first = 1.0 / (16.0 * math.sqrt(grid_size))
    scale_second = 1.0 / math.sqrt(grid_size)
    pieces = []
    for block_index in range(grid_size // block_width):
        cos_table, sin_table = dft_tables(block_index * block_width, block_width, grid_size)
        with_cos = jnp.einsum("kv,xv->kx", cos_table, uv_plane, preferred_element_type=jnp.float32)
        with_sin = jnp.einsum("kv,xv->kx", sin_table, uv_plane, preferred_element_type=jnp.float32)
        real_part = with_cos[:, :strip_rows] - with_sin[:, strip_rows:]
        imag_part = with_sin[:, :strip_rows] + with_cos[:, strip_rows:]
        pieces.append(
            (jnp.concatenate([real_part, imag_part], axis=1) * scale_first).astype(jnp.bfloat16)
        )
    spectrum = jnp.concatenate(pieces, axis=0).reshape(
        owner_count, grid_size // owner_count, 2 * strip_rows
    )
    received = lax.all_to_all(spectrum, "uv", split_axis=0, concat_axis=0, tiled=True)
    sources = received.shape[0]
    item_count = received.shape[1]
    separated = received.reshape(sources, item_count, 2, received.shape[2] // 2)
    outputs = []
    for block_index in range(grid_size // block_width):
        cos_table, sin_table = dft_tables(block_index * block_width, block_width, grid_size)
        cos_blocks = cos_table.reshape(block_width, sources, -1)
        sin_blocks = sin_table.reshape(block_width, sources, -1)
        with_cos = jnp.einsum(
            "smru,lsu->rml", separated, cos_blocks, preferred_element_type=jnp.float32
        )
        with_sin = jnp.einsum(
            "smru,lsu->rml", separated, sin_blocks, preferred_element_type=jnp.float32
        )
        real_part = (with_cos[0] - with_sin[1]) * scale_second
        imag_part = (with_sin[0] + with_cos[1]) * scale_second
        outputs.append(jnp.stack([real_part, imag_part]))
    picture_rows = jnp.concatenate(outputs, axis=2)
    return picture_rows[None]


def solution(mesh):
    return jax.shard_map(
        on_device,
        mesh=mesh,
        in_specs=(
            P(("groups", "chan", "pol"), "uv", None, None),
            P(("groups", "uv"), None, None),
            P(("groups", "chan", "pol"), "uv", None),
            P(("groups", "chan", "pol"), "uv"),
            P(("groups", "chan", "pol"), None, None),
            P(),
            P(),
        ),
        out_specs=P(("groups", "chan", "pol"), None, "uv", None),
        check_vma=False,
    )
```

profile of v0, /device:TPU:0, one launch (start us, length us, event | category | flops | bytes accessed | tf_op | source)
XLA Modules:
  0.0 613.5 jit_solution(17508883280715205343)
XLA Ops:
  0.0 0.7 fusion.150
  0.8 0.8 select_reduce_fusion.1
  2.3 0.7 select_reduce_fusion
  3.7 6.3 %all-to-all-start = ((s32[4,32,1]{1,2,0:T(1,128)}), s32[4,32,1]{1,2,0:T(1,128)S(1)}, u32[]{:S(2)}, u32[]{:S(2)}) async-start(s32[4,32,1]{1,2,0:T(1,128)} %bitcast.13), calls=%async_computation | async-start | bytes 4096 | tf_op jit(solution)/shard_map/all_to_all | solution.py:108
  10.1 0.8 fusion.217
  10.8 1.0 copy.46
  11.8 1.0 fusion.216
  13.6 28.5 %while.10 = (s32[]{:T(128)}, f32[8,8,64,128]{3,2,1,0:T(8,128)S(1)}, s32[8,8,128]{2,1,0:T(8,128)S(1)}, f32[256,130]{0,1:T(8,128)S(1)}, s32[8,8,128]{2,1,0:T(8,128...) while((s32[]{:T(128)}, f32[8,8,64,128]{3,2,1,0:T(8,128)S(1)}, s32[8,8,128]{2,1,0:T(8,128)S(1)}, ...), condition=%wide.region_4.5_spmd, body=%wide.region_3.4_spmd.sunk | while | flops 919484416 | bytes 4857945 | solution.py:102
  13.6 0.8 fusion.245
  14.3 0.8 fusion.246
  16.0 1.1 fusion.247
  17.2 0.7 fusion.245
  17.9 0.8 fusion.246
  19.6 1.1 fusion.247
  20.7 0.7 fusion.245
  21.5 0.7 fusion.246
  23.1 1.1 fusion.247
  24.3 0.7 fusion.245
  25.0 0.8 fusion.246
  26.7 1.1 fusion.247
  27.8 0.7 fusion.245
  28.6 0.7 fusion.246
  29.4 0.7 constant_dynamic-slice_fusion.2
  30.2 1.1 fusion.247
  31.4 0.7 fusion.245
  32.2 0.8 fusion.246
  33.8 1.1 fusion.247
  35.0 0.7 fusion.245
  35.7 0.7 fusion.246
  37.4 1.1 fusion.247
  38.5 0.7 fusion.245
  39.3 0.8 fusion.246
  40.9 1.1 fusion.247
  42.1 4.6 fusion.88
  46.7 4.4 copy.50
  51.1 5.3 all-to-all-start.1
  57.1 0.7 reduce.3
  57.9 91.5 %all-to-all-done.1 = f32[128,64,128]{2,1,0:T(8,128)} async-done(((f32[128,64,128]{2,1,0:T(8,128)}), f32[128,64,128]{2,1,0:T(8,128)}, u32[]{:S(2)}, u32[]{:S(2)}) %all-to-all-start.1) | async-done | bytes 4194336 | tf_op jit(solution)/shard_map/all_to_all | solution.py:107
  149.4 13.0 %fusion.53 = bf16[256,64,128]{2,0,1:T(8,128)(2,1)} fusion(f32[128,64,128]{2,1,0:T(8,128)} %all-to-all-done.1, s32[128]{0:T(128)S(1)} %eq.86), kind=kOutput, calls=%fused_computation.118 | convolution fusion | flops 3223355392 | bytes 8389120 | tf_op jit(solution)/shard_map/sc,sax->cax/dot_general | solution.py:61
  162.4 14.7 %convert_element_type.279 = bf16[8,32,64,2,64]{4,3,1,0,2:T(2,128)(2,1)} reshape(bf16[256,64,128]{2,0,1:T(8,128)(2,1)} %fusion.53) | data formatting | bytes 8388608 | tf_op jit(solution)/shard_map/convert_element_type | solution.py:114
  177.0 8.2 %copy.107 = bf16[8,32,64,2,64]{4,1,2,0,3:T(8,128)(2,1)} copy(bf16[8,32,64,2,64]{4,3,1,0,2:T(2,128)(2,1)} %convert_element_type.279) | data formatting | bytes 8388608 | tf_op jit(solution)/shard_map/convert_element_type | solution.py:114
  185.3 12.7 %convert_element_type.281 = bf16[1024,2048]{1,0:T(8,128)(2,1)} reshape(bf16[2,8,64,32,64]{4,3,2,1,0:T(8,128)(2,1)} %bitcast.212) | data formatting | bytes 8388608 | tf_op jit(solution)/shard_map/convert_element_type | solution.py:114
  198.0 19.2 %fusion.61 = f32[512,1024]{1,0:T(8,128)S(1)} fusion(bf16[1024,2048]{1,0:T(8,128)(2,1)} %convert_element_type.281, s32[512]{0:T(512)S(1)} %iota_add_fusion.2), kind=kOutput, calls=%fused_computation.123 | convolution fusion | flops 2163212288 | bytes 6293504 | tf_op jit(solution)/shard_map/kv,xv->kx/dot_general | solution.py:121
  217.2 17.0 %fusion.62 = f32[512,1024]{1,0:T(8,128)S(1)} fusion(bf16[1024,2048]{1,0:T(8,128)(2,1)S(1)} %copy-done, s32[512]{0:T(512)S(1)} %iota_add_fusion.2), kind=kOutput, calls=%fused_computation.124 | convolution fusion | flops 2163212288 | bytes 6293504 | tf_op jit(solution)/shard_map/kv,xv->kx/dot_general | solution.py:122
  234.2 17.3 %fusion.59 = f32[512,1024]{1,0:T(8,128)S(1)} fusion(bf16[1024,2048]{1,0:T(8,128)(2,1)S(1)} %copy-done), kind=kOutput, calls=%fused_computation.121 | convolution fusion | flops 2163212288 | bytes 6291456 | tf_op jit(solution)/shard_map/kv,xv->kx/dot_general | solution.py:121
  251.5 17.1 %fusion.60 = f32[512,1024]{1,0:T(8,128)S(1)} fusion(bf16[1024,2048]{1,0:T(8,128)(2,1)S(1)} %copy-done), kind=kOutput, calls=%fused_computation.122 | convolution fusion | flops 2163212288 | bytes 6291456 | tf_op jit(solution)/shard_map/kv,xv->kx/dot_general | solution.py:122
  268.6 17.2 %fusion.65 = f32[512,1024]{1,0:T(8,128)S(1)} fusion(bf16[1024,2048]{1,0:T(8,128)(2,1)S(1)} %copy-done, s32[512]{0:T(512)S(1)} %iota_add_fusion), kind=kOutput, calls=%fused_computation.127 | convolution fusion | flops 2163212288 | bytes 6293504 | tf_op jit(solution)/shard_map/kv,xv->kx/dot_general | solution.py:121
  285.8 17.0 %fusion.66 = f32[512,1024]{1,0:T(8,128)S(1)} fusion(bf16[1024,2048]{1,0:T(8,128)(2,1)S(1)} %copy-done, s32[512]{0:T(512)S(1)} %iota_add_fusion), kind=kOutput, calls=%fused_computation.128 | convolution fusion | flops 2163212288 | bytes 6293504 | tf_op jit(solution)/shard_map/kv,xv->kx/dot_general | solution.py:122
  302.8 17.1 %fusion.63 = f32[512,1024]{1,0:T(8,128)S(1)} fusion(bf16[1024,2048]{1,0:T(8,128)(2,1)S(1)} %copy-done, s32[512]{0:T(512)S(1)} %iota_add_fusion.1), kind=kOutput, calls=%fused_computation.125 | convolution fusion | flops 2163212288 | bytes 6293504 | tf_op jit(solution)/shard_map/kv,xv->kx/dot_general | solution.py:121
  319.8 17.2 %fusion.64 = f32[512,1024]{1,0:T(8,128)S(1)} fusion(bf16[1024,2048]{1,0:T(8,128)(2,1)S(1)} %copy-done, s32[512]{0:T(512)S(1)} %iota_add_fusion.1), kind=kOutput, calls=%fused_computation.126 | convolution fusion | flops 2163212288 | bytes 6293504 | tf_op jit(solution)/shard_map/kv,xv->kx/dot_general | solution.py:122
  340.1 2.3 pad_maximum_fusion
  342.4 6.3 %copy.53 = bf16[4,512,1024]{1,2,0:T(8,128)(2,1)} copy(bf16[4,512,1024]{2,1,0:T(8,128)(2,1)} %bitcast.213) | data formatting | bytes 8388608 | tf_op jit(solution)/shard_map/reshape | solution.py:128
  348.6 5.2 all-to-all-start.2
  353.9 92.3 %all-to-all-done.2 = bf16[4,512,1024]{1,2,0:T(8,128)(2,1)} async-done(((bf16[4,512,1024]{1,2,0:T(8,128)(2,1)}), bf16[4,512,1024]{1,2,0:T(8,128)(2,1)}, u32[]{:S(2)}, u32[]{:S(2)}) %all-to-all-start.2) | async-done | bytes 4194336 | tf_op jit(solution)/shard_map/all_to_all | solution.py:131
  446.2 19.0 %fusion.129 = f32[2,512,512]{1,2,0:T(8,128)S(1)} fusion(bf16[4,512,2,512]{1,3,2,0:T(8,128)(2,1)} %bitcast.26, s32[4,512]{1,0:T(4,128)S(1)} %multiply_add_fusion.2), kind=kOutput, calls=%fused_computation.161 | convolution fusion | flops 2163212288 | bytes 6299648 | tf_op jit(solution)/shard_map/smru,lsu->rml/dot_general | solution.py:143
  465.2 18.9 %fusion.132 = f32[2,512,512]{1,2,0:T(8,128)S(1)} fusion(bf16[4,512,2,512]{1,3,2,0:T(8,128)(2,1)} %bitcast.26, s32[4,512]{1,0:T(4,128)S(1)} %multiply_add_fusion.2), kind=kOutput, calls=%fused_computation.162 | convolution fusion | flops 2163212288 | bytes 6299648 | tf_op jit(solution)/shard_map/smru,lsu->rml/dot_general | solution.py:140
  484.1 19.4 %fusion.123 = f32[2,512,512]{1,2,0:T(8,128)S(1)} fusion(bf16[4,512,2,512]{1,3,2,0:T(8,128)(2,1)} %bitcast.26, s32[4,512]{1,0:T(4,128)S(1)} %multiply_add_fusion.2, s32[512]{0:T(512)S(1)} %iota_add_fusion.2), kind=kOutput, calls=%fused_computation.159 | convolution fusion | flops 2163212288 | bytes 6301696 | tf_op jit(solution)/shard_map/smru,lsu->rml/dot_general | solution.py:143
  503.5 18.8 %fusion.126 = f32[2,512,512]{1,2,0:T(8,128)S(1)} fusion(bf16[4,512,2,512]{1,3,2,0:T(8,128)(2,1)} %bitcast.26, s32[4,512]{1,0:T(4,128)S(1)} %multiply_add_fusion.2, s32[512]{0:T(512)S(1)} %iota_add_fusion.2), kind=kOutput, calls=%fused_computation.160 | convolution fusion | flops 2163212288 | bytes 6301696 | tf_op jit(solution)/shard_map/smru,lsu->rml/dot_general | solution.py:140
  522.3 19.2 %fusion.117 = f32[2,512,512]{1,2,0:T(8,128)S(1)} fusion(bf16[4,512,2,512]{1,3,2,0:T(8,128)(2,1)} %bitcast.26, s32[4,512]{1,0:T(4,128)S(1)} %multiply_add_fusion.2, s32[512]{0:T(512)S(1)} %iota_add_fusion.1), kind=kOutput, calls=%fused_computation.157 | convolution fusion | flops 2163212288 | bytes 6301696 | tf_op jit(solution)/shard_map/smru,lsu->rml/dot_general | solution.py:143
  541.5 19.0 %fusion.120 = f32[2,512,512]{1,2,0:T(8,128)S(1)} fusion(bf16[4,512,2,512]{1,3,2,0:T(8,128)(2,1)} %bitcast.26, s32[4,512]{1,0:T(4,128)S(1)} %multiply_add_fusion.2, s32[512]{0:T(512)S(1)} %iota_add_fusion.1), kind=kOutput, calls=%fused_computation.158 | convolution fusion | flops 2163212288 | bytes 6301696 | tf_op jit(solution)/shard_map/smru,lsu->rml/dot_general | solution.py:140
  560.5 19.0 %fusion.114 = f32[2,512,512]{1,2,0:T(8,128)S(1)} fusion(bf16[4,512,2,512]{1,3,2,0:T(8,128)(2,1)} %bitcast.26, s32[4,512]{1,0:T(4,128)S(1)} %multiply_add_fusion.2, s32[512]{0:T(512)S(1)} %iota_add_fusion), kind=kOutput, calls=%fused_computation.156 | convolution fusion | flops 2163212288 | bytes 6301696 | tf_op jit(solution)/shard_map/smru,lsu->rml/dot_general | solution.py:140
  579.6 19.2 %fusion.111 = f32[2,512,512]{1,2,0:T(8,128)S(1)} fusion(bf16[4,512,2,512]{1,3,2,0:T(8,128)(2,1)} %bitcast.26, s32[4,512]{1,0:T(4,128)S(1)} %multiply_add_fusion.2, s32[512]{0:T(512)S(1)} %iota_add_fusion), kind=kOutput, calls=%fused_computation.155 | convolution fusion | flops 2163212288 | bytes 6301696 | tf_op jit(solution)/shard_map/smru,lsu->rml/dot_general | solution.py:143
  600.8 3.8 maximum_bitcast_fusion
  604.6 8.7 %copy.62 = f32[1,2,512,2048]{3,2,1,0:T(8,128)} copy(f32[1,2,512,2048]{2,3,1,0:T(8,128)} %maximum_bitcast_fusion) | data formatting | bytes 16777216 | tf_op jit(solution)/shard_map/broadcast_in_dim | solution.py:150
  (90 shorter events, 14.0 us)
Async XLA Ops:
  3.7 47.4 %all-to-all-start = ((s32[4,32,1]{1,2,0:T(1,128)}), s32[4,32,1]{1,2,0:T(1,128)S(1)}, u32[]{:S(2)}, u32[]{:S(2)}) async-start(s32[4,32,1]{1,2,0:T(1,128)} %bitcast.13), calls=%async_computation | async-start | bytes 4096 | tf_op jit(solution)/shard_map/all_to_all | solution.py:108
  51.1 98.3 %all-to-all-start.1 = ((f32[128,64,128]{2,1,0:T(8,128)}), f32[128,64,128]{2,1,0:T(8,128)}, u32[]{:S(2)}, u32[]{:S(2)}) async-start(f32[128,64,128]{2,1,0:T(8,128)} %copy.50), calls=%async_computation.1 | async-start | bytes 8388608 | tf_op jit(solution)/shard_map/all_to_all | solution.py:107
  198.0 19.2 %copy-start = (bf16[1024,2048]{1,0:T(8,128)(2,1)S(1)}, bf16[1024,2048]{1,0:T(8,128)(2,1)}, u32[]{:S(2)}) copy-start(bf16[1024,2048]{1,0:T(8,128)(2,1)} %convert_element_type.281) | copy-start | bytes 12582916
  348.6 97.5 %all-to-all-start.2 = ((bf16[4,512,1024]{1,2,0:T(8,128)(2,1)}), bf16[4,512,1024]{1,2,0:T(8,128)(2,1)}, u32[]{:S(2)}, u32[]{:S(2)}) async-start(bf16[4,512,1024]{1,2,0:T(8,128)(2,1)} %copy.53), calls=%async_computation.2 | async-start | bytes 8388608 | tf_op jit(solution)/shard_map/all_to_all | solution.py:131
where the time goes:
time: 623 us; the launch traced here: 614 us
  matrix products  330 us (53%)
  waiting for transfers between devices  184 us (30%)
  local copies, waits for them, and re-layouts  64.8 us (10%)
  starting transfers between devices  16.9 us (3%)
  other arithmetic  16.8 us (3%)
    all_to_all x1, waiting for transfers between devices, on_device(): lax.all_to_all(spectrum, 'uv', split_axis=0, concat_axis=0, tiled=True)  92.3 us
    all_to_all x1, waiting for transfers between devices, on_device(): lax.all_to_all(outgoing, 'uv', split_axis=0, concat_axis=0, tiled=True)  91.5 us
    dot_general x4, matrix products, on_device(): jnp.einsum('smru,lsu->rml', separated, sin_blocks, preferred_element_type...  76.7 us
    dot_general x4, matrix products, on_device(): jnp.einsum('smru,lsu->rml', separated, cos_blocks, preferred_element_type...  75.8 us
    dot_general x4, matrix products, on_device(): jnp.einsum('kv,xv->kx', cos_table, uv_plane, preferred_element_type=jnp.f...  70.7 us
    dot_general x4, matrix products, on_device(): jnp.einsum('kv,xv->kx', sin_table, uv_plane, preferred_element_type=jnp.f...  68.2 us
    convert_element_type x3, local copies, waits for them, and re-layouts, on_device(): uv_plane = uv_plane.reshape(2 * strip_rows, grid_size).astype(jnp.bfloat16)  35.6 us
    dot_general x1, matrix products, place_cells(): jnp.einsum('sc,sax->cax', deposited_cells, sub_grids, precision=lax.Preci...  13 us
  transfers between devices with their start and end apart: 3, of which 2 were waited for; matrix products, arithmetic and copies ran while one was open for 7% of the time, Pallas kernels for 0%

commit v1 on v0

v1 whole, which is shorter than its diff:
```python
import functools
import math

import jax
import jax.numpy as jnp
import ml_dtypes
import numpy as np
from jax import lax
from jax.experimental import pallas as pl
from jax.experimental.pallas import tpu as pltpu
from jax.sharding import PartitionSpec as P

GRID = 2048
KERN = 64
COLS = GRID // KERN
QUAD = 4
BATCH = 8
LIMIT = 60 * 1024 * 1024
BF = jnp.bfloat16
F32 = jnp.float32


@functools.lru_cache(maxsize=None)
def full_tables():
    index = np.arange(GRID)
    angles = 2.0 * np.pi * ((index[:, None] * index[None, :]) % GRID) / GRID
    return (
        np.cos(angles).astype(np.float32).astype(ml_dtypes.bfloat16),
        np.sin(angles).astype(np.float32).astype(ml_dtypes.bfloat16),
    )


@functools.lru_cache(maxsize=None)
def quad_table():
    cos_table, sin_table = full_tables()
    quarter = GRID // QUAD
    rows = np.arange(GRID).reshape(COLS, KERN // QUAD, QUAD)
    out = np.zeros((QUAD, COLS, 2, KERN // QUAD, 2, quarter), ml_dtypes.bfloat16)
    for r in range(QUAD):
        c = cos_table[rows[:, :, r], :quarter]
        s = sin_table[rows[:, :, r], :quarter]
        out[r, :, 0, :, 0] = c
        out[r, :, 1, :, 0] = -s
        out[r, :, 0, :, 1] = s
        out[r, :, 1, :, 1] = c
    return out.reshape(QUAD, GRID // 2, GRID // 2)


def grid_kernel(steps, place_ref, vis_ref, pair_ref, table_ref, plane_ref, total):
    step = pl.program_id(0)

    @pl.when(step == 0)
    def _():
        @pl.loop(0, COLS)
        def _(col):
            total[col] = jnp.zeros((COLS, KERN, 2 * KERN), F32)

    @pl.when(step < steps)
    def _():
        tiles = table_ref.shape[1]
        tile_number = lax.broadcasted_iota(jnp.int32, (tiles, 256), 0)
        table = table_ref[...]
        for j in range(BATCH):
            pair = jnp.concatenate(
                [pair_ref[2 * j : 2 * j + 1, :], pair_ref[2 * j + 1 : 2 * j + 2, :]], axis=1
            )
            chosen = jnp.where(tile_number == pair, 1.0, 0.0).astype(BF)
            rows = jnp.dot(table, chosen, preferred_element_type=F32)
            both = rows[:128] + rows[128:256]
            kernels = both[:, :128] * both[:, 128:]
            ku, kv = kernels[:64], kernels[64:]
            real = rows[256:257] + rows[257:258] + rows[258:259]
            imag = rows[259:260] + rows[260:261] + rows[261:262]
            sr, tr, si, ti = real[:, :128], real[:, 128:], imag[:, :128], imag[:, 128:]
            vr, vi = vis_ref[2 * j : 2 * j + 1, :], vis_ref[2 * j + 1 : 2 * j + 2, :]
            pr = sr * vr - si * vi
            pi = sr * vi + si * vr
            gr = pr * tr + pi * ti
            gi = pi * tr - pr * ti
            weighted = []
            for r in range(QUAD):
                band = ku[16 * r : 16 * r + 16]
                weighted += [gr * band, gi * band]
            weighted = jnp.concatenate(weighted, axis=0)
            w_high = weighted.astype(BF)
            w_low = (weighted - w_high.astype(F32)).astype(BF)
            v_high = kv.astype(BF)
            v_low = (kv - v_high.astype(F32)).astype(BF)
            product = lax.dot_general(
                jnp.concatenate([v_high, v_low], axis=0),
                jnp.concatenate([w_high, w_low], axis=0),
                (((1,), (1,)), ((), ())),
                preferred_element_type=F32,
            )
            cell = product[:64, :128] + (
                product[64:, :128] + product[:64, 128:] + product[64:, 128:]
            )
            where = place_ref[step * BATCH + j]
            total[where // COLS, where % COLS] += cell

    @pl.when(step >= steps)
    def _():
        first = (step - steps) * 2

        for half in range(2):
            for row in range(COLS):
                plane_ref[half * KERN : (half + 1) * KERN, row * 128 : (row + 1) * 128] = total[
                    first + half, row
                ].astype(BF)


def grid_plane(places, vis, pairs, table):
    nblocks = places.shape[0]
    steps = nblocks // BATCH
    rows = table.shape[0]
    tiles = table.shape[1]
    return pl.pallas_call(
        functools.partial(grid_kernel, steps),
        out_shape=jax.ShapeDtypeStruct((GRID, 2 * GRID), BF),
        grid_spec=pltpu.PrefetchScalarGridSpec(
            num_scalar_prefetch=1,
            grid=(steps + COLS // 2,),
            in_specs=[
                pl.BlockSpec((2 * BATCH, 128), lambda i, p: (jnp.minimum(i, steps - 1), 0)),
                pl.BlockSpec((2 * BATCH, 128), lambda i, p: (jnp.minimum(i, steps - 1), 0)),
                pl.BlockSpec((rows, tiles), lambda i, p: (0, 0)),
            ],
            out_specs=pl.BlockSpec((128, 2 * GRID), lambda i, p: (jnp.maximum(i - steps, 0), 0)),
            scratch_shapes=[pltpu.VMEM((COLS, COLS, KERN, 2 * KERN), F32)],
        ),
        compiler_params=pltpu.CompilerParams(vmem_limit_bytes=LIMIT),
    )(places, vis, pairs, table)


def image_kernel(band, tile, me_ref, cos_ref, sin_ref, plane_ref, quad_ref, image_ref, spectrum):
    step = pl.program_id(0)
    groups = COLS // 4
    scale_first = 1.0 / (16.0 * math.sqrt(GRID))
    scale_second = 1.0 / math.sqrt(GRID)
    quarter = GRID // QUAD

    @pl.when(step < groups)
    def _():
        data = plane_ref[...]
        lane = lax.broadcasted_iota(jnp.int32, (tile, 512), 1) % 32
        for top in range(0, band, tile):
            with_cos = jnp.dot(cos_ref[top : top + tile, :], data, preferred_element_type=F32)
            with_sin = jnp.dot(sin_ref[top : top + tile, :], data, preferred_element_type=F32)
            swapped = jnp.where(
                lane < 16, -pltpu.roll(with_sin, 512 - 16, 1), pltpu.roll(with_sin, 16, 1)
            )
            mixed = (with_cos + swapped) * scale_first
            for r in range(QUAD):
                picked = jnp.concatenate(
                    [mixed[:, 128 * k + 32 * r : 128 * k + 32 * r + 32] for k in range(4)], axis=1
                )
                spectrum[r, top : top + tile, pl.ds(pl.multiple_of(step * 128, 128), 128)] = (
                    picked.astype(BF)
                )

    @pl.when(step >= groups)
    def _():
        top = pl.multiple_of((step - groups) * tile, tile)
        for left in range(0, quarter, 256):
            real, imag = [], []
            for r in range(QUAD):
                part = spectrum[r, pl.ds(top, tile), :]
                real.append(
                    jnp.dot(part, quad_ref[r, :, left : left + 256], preferred_element_type=F32)
                )
                imag.append(
                    jnp.dot(
                        part,
                        quad_ref[r, :, quarter + left : quarter + left + 256],
                        preferred_element_type=F32,
                    )
                )
            er, ei = real[0] + real[2], imag[0] + imag[2]
            fr, fi = real[0] - real[2], imag[0] - imag[2]
            gr, gi = real[1] + real[3], imag[1] + imag[3]
            hr, hi = real[1] - real[3], imag[1] - imag[3]
            parts = [
                (er + gr, ei + gi),
                (fr - hi, fi + hr),
                (er - gr, ei - gi),
                (fr + hi, fi - hr),
            ]
            for q in range(QUAD):
                at = q * quarter + left
                image_ref[0, 0, :, at : at + 256] = parts[q][0] * scale_second
                image_ref[0, 1, :, at : at + 256] = parts[q][1] * scale_second


def make_image(me, plane, band):
    cos_table, sin_table = full_tables()
    tile = min(256, band)
    groups = COLS // 4
    return pl.pallas_call(
        functools.partial(image_kernel, band, tile),
        out_shape=jax.ShapeDtypeStruct((1, 2, band, GRID), F32),
        grid_spec=pltpu.PrefetchScalarGridSpec(
            num_scalar_prefetch=1,
            grid=(groups + band // tile,),
            in_specs=[
                pl.BlockSpec((band, GRID), lambda i, m: (m[0], 0)),
                pl.BlockSpec((band, GRID), lambda i, m: (m[0], 0)),
                pl.BlockSpec((GRID, 512), lambda i, m: (0, jnp.minimum(i, groups - 1))),
                pl.BlockSpec((QUAD, GRID // 2, GRID // 2), lambda i, m: (0, 0, 0)),
            ],
            out_specs=pl.BlockSpec(
                (1, 2, tile, GRID), lambda i, m: (0, 0, jnp.maximum(i - groups, 0), 0)
            ),
            scratch_shapes=[pltpu.VMEM((QUAD, band, GRID // 2), BF)],
        ),
        compiler_params=pltpu.CompilerParams(vmem_limit_bytes=LIMIT),
    )(me, jnp.asarray(cos_table), jnp.asarray(sin_table), plane, jnp.asarray(quad_table()))


def rounded(x):
    return lax.reduce_precision(x, exponent_bits=8, mantissa_bits=7)


def lookup_rows(beams, support, gains):
    half = beams.shape[1] // 2
    width = half // 4
    masked = beams * jnp.repeat(support, width, axis=1).astype(F32)
    by_column = masked.T
    along_u = by_column[:half].reshape(half // QUAD, QUAD, -1).transpose(1, 0, 2).reshape(half, -1)
    values = jnp.concatenate([along_u, by_column[half:]], axis=0)
    high = rounded(values)
    low = values - high
    gain_high = rounded(gains)
    rest = gains - gain_high
    gain_mid = rounded(rest)
    gain_low = rest - gain_mid
    gain_rows = jnp.stack([gain_high, gain_mid, gain_low], axis=1).reshape(6, -1)
    blank = jnp.zeros((10, gains.shape[1]), F32)
    return jnp.concatenate([high, low, gain_rows, blank], axis=0).astype(BF)


def on_device(visibilities, tile_pairs, owner_tiles, cell_ids, gains, beams, support):
    owners = lax.axis_size("uv")
    me = lax.axis_index("uv").astype(jnp.int32).reshape(1)
    nblocks, _, rows_each = visibilities.shape[1:]
    band = GRID // owners
    bands_each = band // KERN
    lines = 2 * nblocks * rows_each // 128
    meta = jnp.concatenate([owner_tiles[0, :, 0], cell_ids[0]]).reshape(-1, 128)
    meta = jnp.pad(meta, ((0, 16 - meta.shape[0]), (0, 0)))
    packed = jnp.concatenate(
        [
            visibilities.reshape(lines, 128),
            tile_pairs.reshape(lines, 128).astype(BF),
            meta.astype(BF),
        ],
        axis=0,
    )
    gathered = lax.all_gather(packed, "uv", axis=0, tiled=False)
    vis = gathered[:, :lines].reshape(owners * lines, 128).astype(F32)
    pairs = gathered[:, lines : 2 * lines].reshape(owners * lines, 128).astype(jnp.int32)
    notes = gathered[:, 2 * lines : 2 * lines + 2 * nblocks // 128].reshape(owners, 2, nblocks)
    notes = notes.astype(jnp.int32)
    cells = notes[:, 1]
    places = (cells % COLS) * COLS + notes[:, 0] * bands_each + cells // COLS
    table = lookup_rows(beams, support, gains[0])
    plane = grid_plane(places.reshape(-1), vis, pairs, table)
    return make_image(me, plane, band)


def solution(mesh):
    return jax.shard_map(
        on_device,
        mesh=mesh,
        in_specs=(
            P(("groups", "chan", "pol"), "uv", None, None),
            P(("groups", "uv"), None, None),
            P(("groups", "chan", "pol"), "uv", None),
            P(("groups", "chan", "pol"), "uv"),
            P(("groups", "chan", "pol"), None, None),
            P(),
            P(),
        ),
        out_specs=P(("groups", "chan", "pol"), None, "uv", None),
        check_vma=False,
    )
```

time: 623 us -> 146 us (0.23); the launches traced: 614 us -> 145 us
  matrix products: 330 us -> 0 us
  waiting for transfers between devices: 184 us -> 0 us
  Pallas kernels: 0 us -> 121 us
  local copies, waits for them, and re-layouts: 64.8 us -> 1.41 us
  starting transfers between devices: 16.9 us -> 0 us
  blocking collectives: 0 us -> 15.6 us
  other arithmetic: 16.8 us -> 6.67 us
    dot_general x42 -> x0, matrix products: 330 us -> none  [the longest x4 76.7 us: on_device(): jnp.einsum('smru,lsu->rml', separated, sin_blocks, preferred_element_type...]
    all_to_all x3 -> x0, waiting for transfers between devices: 184 us -> none  [the longest x1 92.3 us: on_device(): lax.all_to_all(spectrum, 'uv', split_axis=0, concat_axis=0, tiled=True)]
    pallas_call x0 -> x2, Pallas kernels: none -> 121 us  [the longest x1 87.7 us: grid_plane(): pl.pallas_call(functools.partial(grid_kernel, steps), out_shape=jax.Shape...]
    convert_element_type x3 -> x1, local copies, waits for them, and re-layouts: 35.6 us -> 0.08 us  [on_device(): notes = notes.astype(jnp.int32)]
    all_to_all x3 -> x0, starting transfers between devices: 16.9 us -> none  [the longest x1 6.32 us: on_device(): lax.all_to_all(slot_cells, 'uv', split_axis=0, concat_axis=0, tiled=True)]
    all_gather x0 -> x1, blocking collectives: none -> 15.6 us  [on_device(): gathered = lax.all_gather(packed, 'uv', axis=0, tiled=False)]
    broadcast_in_dim x3 -> x1, local copies, waits for them, and re-layouts: 8.68 us -> 0.01 us  [lookup_rows(): blank = jnp.zeros((10, gains.shape[1]), F32)]
    reshape x1 -> x2, local copies, waits for them, and re-layouts: 6.29 us -> 0.04 us  [the longest x1 0.02 us: lookup_rows(): by_column[:half].reshape(half // QUAD, QUAD, -1).transpose(1, 0, 2)]
  transfers between devices with their start and end apart: 3 -> 0, of which waited for: 2 -> 0; matrix products, arithmetic and copies ran while one was open for 7% -> 0% of each run, Pallas kernels for 0% -> 0%
where the time goes in v1:
time: 146 us; the launch traced here: 145 us
  Pallas kernels  121 us (83%)
  blocking collectives  15.6 us (11%)
  other arithmetic  6.67 us (5%)
    pallas_call x1, Pallas kernels, grid_plane(): pl.pallas_call(functools.partial(grid_kernel, steps), out_shape=jax.Shape...  87.7 us
    pallas_call x1, Pallas kernels, make_image(): pl.pallas_call(functools.partial(image_kernel, band, tile), out_shape=jax...  33.7 us
    all_gather x1, blocking collectives, on_device(): gathered = lax.all_gather(packed, 'uv', axis=0, tiled=False)  15.6 us

profile of v1, /device:TPU:0, one launch (start us, length us, event | category | flops | bytes accessed | tf_op | source)
XLA Modules:
  0.0 145.2 jit_solution(8565283075284925401)
XLA Ops:
  0.0 0.7 convert_bitcast_fusion.1
  0.7 0.7 convert_bitcast_fusion
  1.3 0.1 maximum_bitcast_fusion
  1.4 0.1 pad.9.clone
  1.5 0.7 reduce-precision_convert_fusion.2
  2.2 0.7 convert_element_type.39
  2.9 0.9 convert_element_type.31
  3.8 0.8 fusion.2
  4.5 1.0 copy.14
  5.7 0.8 maximum_maximum_fusion.table_ref
  6.4 15.6 %all-gather = bf16[1088,128]{1,0:T(8,128)(2,1)S(1)} all-gather(bf16[272,128]{1,0:T(8,128)(2,1)S(1)} %fusion.2), channel_id=2, replica_groups=mesh['groups'=2,'uv'=4,'chan'=2,'pol'=2] {'uv'}, dimensions={0}, use_global_device_ids=true | all-gather | bytes 348160 | tf_op jit(solution)/shard_map/all_gather | solution.py:258
  22.1 0.1 reshape.80
  22.2 0.1 squeeze.17
  22.3 0.1 mul.21
  22.4 0.6 fusion.8.place_ref
  22.9 0.8 bitcast_convert_fusion
  23.8 87.7 %shard_map.100.plane_ref = bf16[2048,4096]{1,0:T(8,128)(2,1)} custom-call(s32[256]{0:T(256)} %fusion.8.place_ref, f32[512,128]{1,0:T(8,128)} %get-tuple-element.17.vis_ref, s32[512,128]{1,0:T(8,128)} %get-tuple-element.16.pair_ref, bf16[272,256]{1,0:T(8,128)(2,1)} %maximum_maximum_fusion.table_ref), custom_call_target="tpu_custom_call" | custom-call | tf_op jit(solution)/shard_map/pallas_call | solution.py:117
  111.5 33.7 %shard_map.101 = f32[1,2,512,2048]{3,2,1,0:T(8,128)} custom-call(s32[1]{0:T(128)} %bitcast.me_ref, bf16[2048,2048]{1,0:T(8,128)(2,1)} %constant.47.clone.cos_ref, bf16[2048,2048]{1,0:T(8,128)(2,1)} %constant.48.clone.sin_ref, bf16[2048,4096]{1,0:T(8,128)(2,1)} %shard_map.100.plane_ref, bf16[4,1024,1024]{2,1,0:T(8,128)(2,1)} %constant.49.clone.quad_ref), custom_call_target="tpu_custom_call" | custom-call | tf_op jit(solution)/shard_map/pallas_call | solution.py:198
  (12 shorter events, 0.2 us)

commit v2 on v1

v2 whole, which is shorter than its diff:
```python
import functools
import math

import jax
import jax.numpy as jnp
import ml_dtypes
import numpy as np
from jax import lax
from jax.experimental import pallas as pl
from jax.experimental.pallas import tpu as pltpu
from jax.sharding import PartitionSpec as P

GRID = 2048
KERN = 64
COLS = GRID // KERN
QUAD = 4
BATCH = 16
LIMIT = 60 * 1024 * 1024
BF = jnp.bfloat16
F32 = jnp.float32


@functools.lru_cache(maxsize=None)
def full_tables():
    index = np.arange(GRID)
    angles = 2.0 * np.pi * ((index[:, None] * index[None, :]) % GRID) / GRID
    return (
        np.cos(angles).astype(np.float32).astype(ml_dtypes.bfloat16),
        np.sin(angles).astype(np.float32).astype(ml_dtypes.bfloat16),
    )


@functools.lru_cache(maxsize=None)
def quad_table():
    cos_table, sin_table = full_tables()
    quarter = GRID // QUAD
    rows = np.arange(GRID).reshape(COLS, KERN // QUAD, QUAD)
    out = np.zeros((QUAD, COLS, 2, KERN // QUAD, 2, quarter), ml_dtypes.bfloat16)
    for r in range(QUAD):
        c = cos_table[rows[:, :, r], :quarter]
        s = sin_table[rows[:, :, r], :quarter]
        out[r, :, 0, :, 0] = c
        out[r, :, 1, :, 0] = -s
        out[r, :, 0, :, 1] = s
        out[r, :, 1, :, 1] = c
    return out.reshape(QUAD, GRID // 2, GRID // 2)


@functools.lru_cache(maxsize=None)
def class_tables(owners):
    cos_table, sin_table = full_tables()
    band = GRID // owners
    order = np.arange(GRID).reshape(owners, band // QUAD, QUAD).transpose(0, 2, 1).reshape(-1)
    quarter = GRID // QUAD
    return cos_table[order, :quarter], sin_table[order, :quarter]


def fused_kernel(
    band, tile, steps,
    place_ref, me_ref, vis_ref, pair_ref, table_ref, cos_ref, sin_ref, quad_hbm,
    image_ref,
    total, chosen, looked, left_rows, right_rows, mixed_cells, woven, spectrum, quad_ref, quad_sem,
):
    step = pl.program_id(0)
    groups = COLS // 4
    quarter = GRID // QUAD
    class_rows = band // QUAD
    scale_first = 1.0 / (16.0 * math.sqrt(GRID))
    scale_second = 1.0 / math.sqrt(GRID)
    quad_copy = pltpu.make_async_copy(quad_hbm, quad_ref, quad_sem)

    @pl.when(step == 0)
    def _():
        quad_copy.start()

        @pl.loop(0, COLS)
        def _(col):
            total[col] = jnp.zeros((COLS, KERN, 2 * KERN), F32)

    @pl.when(step < steps)
    def _():
        tiles = table_ref.shape[1]
        number = lax.broadcasted_iota(jnp.int32, (tiles, 256), 0).astype(F32).astype(BF)
        one, nil = jnp.asarray(1, BF), jnp.asarray(0, BF)
        for j in range(BATCH):
            pair = jnp.concatenate(
                [pair_ref[2 * j : 2 * j + 1, :], pair_ref[2 * j + 1 : 2 * j + 2, :]], axis=1
            )
            pair = jnp.broadcast_to(pair, (16, 256)).astype(BF)
            pair = jnp.concatenate([pair] * (tiles // 16), axis=0)
            chosen[:, j * 256 : (j + 1) * 256] = jnp.where(number == pair, one, nil)
        for j in range(0, BATCH, 2):
            looked[:, j * 256 : (j + 2) * 256] = jnp.dot(
                table_ref[...], chosen[:, j * 256 : (j + 2) * 256], preferred_element_type=F32
            )
        for j in range(BATCH):
            rows = looked[:, j * 256 : (j + 1) * 256]
            both = rows[:128] + rows[128:256]
            kernels = both[:, :128] * both[:, 128:]
            ku, kv = kernels[:64], kernels[64:]
            real = rows[256:257] + rows[257:258] + rows[258:259]
            imag = rows[259:260] + rows[260:261] + rows[261:262]
            sr, tr, si, ti = real[:, :128], real[:, 128:], imag[:, :128], imag[:, 128:]
            vr, vi = vis_ref[2 * j : 2 * j + 1, :], vis_ref[2 * j + 1 : 2 * j + 2, :]
            pr = sr * vr - si * vi
            pi = sr * vi + si * vr
            gr = pr * tr + pi * ti
            gi = pi * tr - pr * ti
            weighted = []
            for r in range(QUAD):
                part = ku[16 * r : 16 * r + 16]
                weighted += [gr * part, gi * part]
            weighted = jnp.concatenate(weighted, axis=0)
            w_high = weighted.astype(BF)
            w_low = (weighted - w_high.astype(F32)).astype(BF)
            v_high = kv.astype(BF)
            v_low = (kv - v_high.astype(F32)).astype(BF)
            left_rows[j] = jnp.concatenate([v_high, v_low], axis=0)
            right_rows[j] = jnp.concatenate([w_high, w_low], axis=0)
        for j in range(BATCH):
            product = lax.dot_general(
                left_rows[j], right_rows[j], (((1,), (1,)), ((), ())), preferred_element_type=F32
            )
            cell = product[:64, :128] + (
                product[64:, :128] + product[:64, 128:] + product[64:, 128:]
            )
            where = place_ref[step * BATCH + j]
            total[where // COLS, where % COLS] += cell

    @pl.when(step == steps)
    def _():
        quad_copy.wait()

    @pl.when((step >= steps) & (step < steps + groups))
    def _():
        group = step - steps
        far = COLS // QUAD

        @pl.loop(0, far)
        def _(col):
            top = pl.multiple_of(col * KERN, KERN)
            lane = lax.broadcasted_iota(jnp.int32, (KERN, 128), 1) % 32
            for k in range(4):
                x = [
                    total[col + far * q, group * 4 + k].astype(BF).astype(F32) for q in range(QUAD)
                ]
                e, f, g, h = x[0] + x[2], x[0] - x[2], x[1] + x[3], x[1] - x[3]
                turned = jnp.where(lane < 16, -pltpu.roll(h, 112, 1), pltpu.roll(h, 16, 1))
                for s, y in enumerate([e + g, f + turned, e - g, f - turned]):
                    mixed_cells[s, pl.ds(top, KERN), k * 128 : (k + 1) * 128] = y.astype(BF)

        lane = lax.broadcasted_iota(jnp.int32, (class_rows, 512), 1) % 32
        for s in range(QUAD):
            mine = slice(s * class_rows, (s + 1) * class_rows)
            data = mixed_cells[s]
            with_cos = jnp.dot(cos_ref[mine, :], data, preferred_element_type=F32)
            with_sin = jnp.dot(sin_ref[mine, :], data, preferred_element_type=F32)
            swapped = jnp.where(
                lane < 16, -pltpu.roll(with_sin, 512 - 16, 1), pltpu.roll(with_sin, 16, 1)
            )
            mixed = (with_cos + swapped) * scale_first
            for r in range(QUAD):
                picked = jnp.concatenate(
                    [mixed[:, 128 * k + 32 * r : 128 * k + 32 * r + 32] for k in range(4)], axis=1
                )
                woven[r, pl.ds(s, class_rows, stride=QUAD), :] = picked
        for r in range(QUAD):
            spectrum[r, :, pl.ds(pl.multiple_of(group * 128, 128), 128)] = woven[r].astype(BF)

    @pl.when(step >= steps + groups)
    def _():
        top = pl.multiple_of((step - steps - groups) * tile, tile)
        for left in range(0, quarter, 256):
            real, imag = [], []
            for r in range(QUAD):
                part = spectrum[r, pl.ds(top, tile), :]
                real.append(
                    jnp.dot(part, quad_ref[r, :, left : left + 256], preferred_element_type=F32)
                )
                imag.append(
                    jnp.dot(
                        part,
                        quad_ref[r, :, quarter + left : quarter + left + 256],
                        preferred_element_type=F32,
                    )
                )
            er, ei = real[0] + real[2], imag[0] + imag[2]
            fr, fi = real[0] - real[2], imag[0] - imag[2]
            gr, gi = real[1] + real[3], imag[1] + imag[3]
            hr, hi = real[1] - real[3], imag[1] - imag[3]
            parts = [
                (er + gr, ei + gi),
                (fr - hi, fi + hr),
                (er - gr, ei - gi),
                (fr + hi, fi - hr),
            ]
            for q in range(QUAD):
                for c in range(2):
                    scaled = parts[q][c] * scale_second
                    image_ref[0, c, :, q * quarter + left : q * quarter + left + 256] = scaled


def make_image(me, places, vis, pairs, table, owners):
    nblocks = places.shape[0]
    steps = nblocks // BATCH
    rows, tiles = table.shape
    band = GRID // owners
    tile = min(128, band)
    groups = COLS // 4
    cos_table, sin_table = class_tables(owners)
    before = steps + groups
    return pl.pallas_call(
        functools.partial(fused_kernel, band, tile, steps),
        out_shape=jax.ShapeDtypeStruct((1, 2, band, GRID), F32),
        grid_spec=pltpu.PrefetchScalarGridSpec(
            num_scalar_prefetch=2,
            grid=(before + band // tile,),
            in_specs=[
                pl.BlockSpec((2 * BATCH, 128), lambda i, p, m: (jnp.minimum(i, steps - 1), 0)),
                pl.BlockSpec((2 * BATCH, 128), lambda i, p, m: (jnp.minimum(i, steps - 1), 0)),
                pl.BlockSpec((rows, tiles), lambda i, p, m: (0, 0)),
                pl.BlockSpec((band, GRID // QUAD), lambda i, p, m: (m[0], 0)),
                pl.BlockSpec((band, GRID // QUAD), lambda i, p, m: (m[0], 0)),
                pl.BlockSpec(memory_space=pl.ANY),
            ],
            out_specs=pl.BlockSpec(
                (1, 2, tile, GRID), lambda i, p, m: (0, 0, jnp.maximum(i - before, 0), 0)
            ),
            scratch_shapes=[
                pltpu.VMEM((COLS, COLS, KERN, 2 * KERN), F32),
                pltpu.VMEM((tiles, BATCH * 256), BF),
                pltpu.VMEM((rows, BATCH * 256), F32),
                pltpu.VMEM((BATCH, 128, 128), BF),
                pltpu.VMEM((BATCH, 256, 128), BF),
                pltpu.VMEM((QUAD, GRID // QUAD, 512), BF),
                pltpu.VMEM((QUAD, band, 128), F32),
                pltpu.VMEM((QUAD, band, GRID // 2), BF),
                pltpu.VMEM((QUAD, GRID // 2, GRID // 2), BF),
                pltpu.SemaphoreType.DMA,
            ],
        ),
        compiler_params=pltpu.CompilerParams(vmem_limit_bytes=LIMIT),
    )(
        places, me, vis, pairs, table,
        jnp.asarray(cos_table), jnp.asarray(sin_table), jnp.asarray(quad_table()),
    )


def rounded(x):
    return lax.reduce_precision(x, exponent_bits=8, mantissa_bits=7)


def lookup_rows(beams, support, gains):
    half = beams.shape[1] // 2
    width = half // 4
    masked = beams * jnp.repeat(support, width, axis=1).astype(F32)
    by_column = masked.T
    along_u = by_column[:half].reshape(half // QUAD, QUAD, -1).transpose(1, 0, 2).reshape(half, -1)
    values = jnp.concatenate([along_u, by_column[half:]], axis=0)
    high = rounded(values)
    low = values - high
    gain_high = rounded(gains)
    rest = gains - gain_high
    gain_mid = rounded(rest)
    gain_low = rest - gain_mid
    gain_rows = jnp.stack([gain_high, gain_mid, gain_low], axis=1).reshape(6, -1)
    blank = jnp.zeros((10, gains.shape[1]), F32)
    return jnp.concatenate([high, low, gain_rows, blank], axis=0).astype(BF)


def on_device(visibilities, tile_pairs, owner_tiles, cell_ids, gains, beams, support):
    owners = lax.axis_size("uv")
    me = lax.axis_index("uv").astype(jnp.int32).reshape(1)
    nblocks, _, rows_each = visibilities.shape[1:]
    band = GRID // owners
    bands_each = band // KERN
    lines = 2 * nblocks * rows_each // 128
    meta = jnp.concatenate([owner_tiles[0, :, 0], cell_ids[0]]).reshape(-1, 128)
    meta = jnp.pad(meta, ((0, 16 - meta.shape[0]), (0, 0)))
    packed = jnp.concatenate(
        [
            visibilities.reshape(lines, 128),
            tile_pairs.reshape(lines, 128).astype(BF),
            meta.astype(BF),
        ],
        axis=0,
    )
    gathered = lax.all_gather(packed, "uv", axis=0, tiled=False)
    vis = gathered[:, :lines].reshape(owners * lines, 128).astype(F32)
    pairs = gathered[:, lines : 2 * lines].reshape(owners * lines, 128).astype(F32)
    notes = gathered[:, 2 * lines : 2 * lines + 2 * nblocks // 128].reshape(owners, 2, nblocks)
    notes = notes.astype(jnp.int32)
    cells = notes[:, 1]
    places = (cells % COLS) * COLS + notes[:, 0] * bands_each + cells // COLS
    table = lookup_rows(beams, support, gains[0])
    return make_image(me, places.reshape(-1), vis, pairs, table, owners)


def solution(mesh):
    return jax.shard_map(
        on_device,
        mesh=mesh,
        in_specs=(
            P(("groups", "chan", "pol"), "uv", None, None),
            P(("groups", "uv"), None, None),
            P(("groups", "chan", "pol"), "uv", None),
            P(("groups", "chan", "pol"), "uv"),
            P(("groups", "chan", "pol"), None, None),
            P(),
            P(),
        ),
        out_specs=P(("groups", "chan", "pol"), None, "uv", None),
        check_vma=False,
    )
```

time: 146 us -> 78.1 us (0.53)
  Pallas kernels: 121 us -> 53.9 us
    pallas_call x2 -> x1, Pallas kernels: 121 us -> 53.9 us  [make_image(): pl.pallas_call(functools.partial(fused_kernel, band, tile, steps), out_sh...]
where the time goes in v2:
time: 78.1 us; the launch traced here: 77.7 us
  Pallas kernels  53.9 us (69%)
  blocking collectives  15.6 us (20%)
  other arithmetic  6.68 us (9%)
  local copies, waits for them, and re-layouts  1.41 us (2%)
    pallas_call x1, Pallas kernels, make_image(): pl.pallas_call(functools.partial(fused_kernel, band, tile, steps), out_sh...  53.9 us
    all_gather x1, blocking collectives, on_device(): gathered = lax.all_gather(packed, 'uv', axis=0, tiled=False)  15.6 us

profile of v2, /device:TPU:0, one launch (start us, length us, event | category | flops | bytes accessed | tf_op | source)
XLA Modules:
  0.0 77.7 jit_solution(1502436872276903345)
XLA Ops:
  0.0 0.7 convert_bitcast_fusion.1
  0.7 0.7 convert_bitcast_fusion
  1.3 0.1 maximum_bitcast_fusion
  1.4 0.1 pad.9.clone
  1.5 0.7 reduce-precision_convert_fusion.2
  2.2 0.7 convert_element_type.39
  2.9 0.9 %convert_element_type.31 = bf16[64,2,128]{2,1,0:T(2,128)(2,1)S(1)} convert(s32[64,2,128]{2,1,0:T(2,128)} %param.11) | non-fusion elementwise | flops 16384 | bytes 98304 | tf_op jit(solution)/shard_map/convert_element_type | solution.py:283
  3.8 0.8 fusion.2
  4.5 1.0 %copy.14 = f32[256,128]{0,1:T(8,128)S(1)} copy(f32[256,128]{1,0:T(8,128)} %param.15) | data formatting | bytes 262144 | tf_op args[5]
  5.7 0.8 maximum_maximum_fusion.table_ref
  6.4 15.6 %all-gather = bf16[1088,128]{1,0:T(8,128)(2,1)S(1)} all-gather(bf16[272,128]{1,0:T(8,128)(2,1)S(1)} %fusion.2), channel_id=2, replica_groups=mesh['groups'=2,'uv'=4,'chan'=2,'pol'=2] {'uv'}, dimensions={0}, use_global_device_ids=true | all-gather | bytes 348160 | tf_op jit(solution)/shard_map/all_gather | solution.py:288
  22.1 0.1 reshape.80
  22.2 0.1 squeeze.17
  22.3 0.1 mul.21
  22.4 0.6 fusion.8.place_ref
  22.9 0.8 %bitcast_convert_fusion = (f32[512,128]{1,0:T(8,128)}, f32[512,128]{1,0:T(8,128)}) fusion(bf16[4,128,128]{2,1,0:T(8,128)(2,1)S(1)} %get-tuple-element.7, bf16[4,128,128]{2,1,0:T(8,128)(2,1)S(1)} %get-tuple-element.8), kind=kLoop, calls=%fused_computation.7 | loop fusion | flops 131072 | bytes 786432 | tf_op jit(solution)/shard_map/convert_element_type | solution.py:290
  23.8 53.9 %shard_map.100 = f32[1,2,512,2048]{3,2,1,0:T(8,128)} custom-call(s32[256]{0:T(256)} %fusion.8.place_ref, s32[1]{0:T(128)} %bitcast.6.me_ref, f32[512,128]{1,0:T(8,128)} %get-tuple-element.17.vis_ref, f32[512,128]{1,0:T(8,128)} %get-tuple-element.16.pair_ref, bf16[272,256]{1,0:T(8,128)(2,1)} %maximum_maximum_fusion.table_ref, ...), custom_call_target="tpu_custom_call" | custom-call | tf_op jit(solution)/shard_map/pallas_call | solution.py:212
  (12 shorter events, 0.2 us)

commit v3 on v2

--- a/solution.py
+++ b/solution.py
@@ -52,12 +52,16 @@
     band = GRID // owners
     order = np.arange(GRID).reshape(owners, band // QUAD, QUAD).transpose(0, 2, 1).reshape(-1)
     quarter = GRID // QUAD
-    return cos_table[order, :quarter], sin_table[order, :quarter]
+    both = np.stack(
+        [table[order, :quarter].reshape(owners, QUAD, -1, quarter) for table in (cos_table, sin_table)],
+        axis=2,
+    )
+    return both.reshape(2 * GRID, quarter)
 
 
 def fused_kernel(
     band, tile, steps,
-    place_ref, me_ref, vis_ref, pair_ref, table_ref, cos_ref, sin_ref, quad_hbm,
+    place_ref, me_ref, vis_ref, pair_ref, table_ref, class_ref, quad_hbm,
     image_ref,
     total, chosen, looked, left_rows, right_rows, mixed_cells, woven, spectrum, quad_ref, quad_sem,
 ):
@@ -98,8 +102,8 @@
             both = rows[:128] + rows[128:256]
             kernels = both[:, :128] * both[:, 128:]
             ku, kv = kernels[:64], kernels[64:]
-            real = rows[256:257] + rows[257:258] + rows[258:259]
-            imag = rows[259:260] + rows[260:261] + rows[261:262]
+            real = rows[256:257] + rows[258:259] + rows[260:261]
+            imag = rows[257:258] + rows[259:260] + rows[261:262]
             sr, tr, si, ti = real[:, :128], real[:, 128:], imag[:, :128], imag[:, 128:]
             vr, vi = vis_ref[2 * j : 2 * j + 1, :], vis_ref[2 * j + 1 : 2 * j + 2, :]
             pr = sr * vr - si * vi
@@ -151,10 +155,9 @@
 
         lane = lax.broadcasted_iota(jnp.int32, (class_rows, 512), 1) % 32
         for s in range(QUAD):
-            mine = slice(s * class_rows, (s + 1) * class_rows)
-            data = mixed_cells[s]
-            with_cos = jnp.dot(cos_ref[mine, :], data, preferred_element_type=F32)
-            with_sin = jnp.dot(sin_ref[mine, :], data, preferred_element_type=F32)
+            mine = slice(2 * s * class_rows, 2 * (s + 1) * class_rows)
+            turned = jnp.dot(class_ref[mine, :], mixed_cells[s], preferred_element_type=F32)
+            with_cos, with_sin = turned[:class_rows], turned[class_rows:]
             swapped = jnp.where(
                 lane < 16, -pltpu.roll(with_sin, 512 - 16, 1), pltpu.roll(with_sin, 16, 1)
             )
@@ -205,9 +208,8 @@
     steps = nblocks // BATCH
     rows, tiles = table.shape
     band = GRID // owners
-    tile = min(128, band)
+    tile = min(256, band)
     groups = COLS // 4
-    cos_table, sin_table = class_tables(owners)
     before = steps + groups
     return pl.pallas_call(
         functools.partial(fused_kernel, band, tile, steps),
@@ -219,8 +221,7 @@
                 pl.BlockSpec((2 * BATCH, 128), lambda i, p, m: (jnp.minimum(i, steps - 1), 0)),
                 pl.BlockSpec((2 * BATCH, 128), lambda i, p, m: (jnp.minimum(i, steps - 1), 0)),
                 pl.BlockSpec((rows, tiles), lambda i, p, m: (0, 0)),
-                pl.BlockSpec((band, GRID // QUAD), lambda i, p, m: (m[0], 0)),
-                pl.BlockSpec((band, GRID // QUAD), lambda i, p, m: (m[0], 0)),
+                pl.BlockSpec((2 * band, GRID // QUAD), lambda i, p, m: (m[0], 0)),
                 pl.BlockSpec(memory_space=pl.ANY),
             ],
             out_specs=pl.BlockSpec(
@@ -242,57 +243,125 @@
         compiler_params=pltpu.CompilerParams(vmem_limit_bytes=LIMIT),
     )(
         places, me, vis, pairs, table,
-        jnp.asarray(cos_table), jnp.asarray(sin_table), jnp.asarray(quad_table()),
-    )
-
-
-def rounded(x):
-    return lax.reduce_precision(x, exponent_bits=8, mantissa_bits=7)
-
-
-def lookup_rows(beams, support, gains):
-    half = beams.shape[1] // 2
-    width = half // 4
-    masked = beams * jnp.repeat(support, width, axis=1).astype(F32)
-    by_column = masked.T
-    along_u = by_column[:half].reshape(half // QUAD, QUAD, -1).transpose(1, 0, 2).reshape(half, -1)
-    values = jnp.concatenate([along_u, by_column[half:]], axis=0)
-    high = rounded(values)
-    low = values - high
-    gain_high = rounded(gains)
+        jnp.asarray(class_tables(owners)), jnp.asarray(quad_table()),
+    )
+
+
+@functools.lru_cache(maxsize=None)
+def row_order():
+    order = np.concatenate(
+        [np.arange(KERN).reshape(-1, QUAD).T.reshape(-1), KERN + np.arange(KERN)]
+    )
+    return np.eye(2 * KERN, dtype=np.float32)[order].astype(ml_dtypes.bfloat16)
+
+
+def gather_kernel(
+    n, lines,
+    vis_ref, pair_ref, meta_ref, beams_ref, support_ref, gains_ref, order_ref,
+    vis_out, pair_out, meta_out, table_out,
+    packed, slots, send_sem, recv_sem,
+):
+    me = lax.axis_index("uv")
+    others = [lax.rem(me + o, n) for o in range(1, n)]
+    barrier = pltpu.get_barrier_semaphore()
+    for other in others:
+        pl.semaphore_signal(
+            barrier, inc=1, device_id={"uv": other}, device_id_type=pl.DeviceIdType.MESH
+        )
+    packed[:lines] = vis_ref[...]
+    packed[lines : 2 * lines] = pair_ref[...].astype(F32).astype(BF)
+    packed[2 * lines :] = meta_ref[...].astype(F32).astype(BF)
+    pl.semaphore_wait(barrier, n - 1)
+    copies = []
+    for o, other in enumerate(others):
+        copy = pltpu.make_async_remote_copy(
+            src_ref=packed,
+            dst_ref=slots.at[me],
+            send_sem=send_sem.at[o],
+            recv_sem=recv_sem.at[o],
+            device_id={"uv": other},
+            device_id_type=pl.DeviceIdType.MESH,
+        )
+        copy.start()
+        copies.append(copy)
+    slots[me] = packed[...]
+    lane = lax.broadcasted_iota(jnp.int32, beams_ref.shape, 1) // (KERN // 4)
+    support = support_ref[...].astype(F32)
+    mask = jnp.zeros(beams_ref.shape, F32)
+    for k in range(8):
+        mask = jnp.where(lane == k, support[:, k : k + 1], mask)
+    masked = beams_ref[...] * mask
+    high = masked.astype(BF)
+    low = (masked - high.astype(F32)).astype(BF)
+    across = (((1,), (1,)), ((), ()))
+    for k, part in enumerate([high, low]):
+        table_out[k * 128 : (k + 1) * 128] = lax.dot_general(
+            order_ref[...], part, across, preferred_element_type=F32
+        ).astype(BF)
+    gains = gains_ref[...]
+    gain_high = gains.astype(BF).astype(F32)
     rest = gains - gain_high
-    gain_mid = rounded(rest)
-    gain_low = rest - gain_mid
-    gain_rows = jnp.stack([gain_high, gain_mid, gain_low], axis=1).reshape(6, -1)
+    gain_mid = rest.astype(BF).astype(F32)
     blank = jnp.zeros((10, gains.shape[1]), F32)
-    return jnp.concatenate([high, low, gain_rows, blank], axis=0).astype(BF)
+    table_out[256:] = jnp.concatenate([gain_high, gain_mid, rest - gain_mid, blank], axis=0).astype(
+        BF
+    )
+    for copy in copies:
+        copy.wait()
+    for i in range(n):
+        vis_out[i * lines : (i + 1) * lines] = slots[i, :lines].astype(F32)
+        pair_out[i * lines : (i + 1) * lines] = slots[i, lines : 2 * lines].astype(F32)
+        meta_out[i] = slots[i, 2 * lines :].astype(F32).astype(jnp.int32)
+
+
+def gather(n, vis, pairs, meta, beams, support, gains):
+    lines = vis.shape[0]
+    extra = meta.shape[0]
+    tiles = beams.shape[0]
+    vmem = pl.BlockSpec(memory_space=pltpu.VMEM)
+    return pl.pallas_call(
+        functools.partial(gather_kernel, n, lines),
+        out_shape=(
+            jax.ShapeDtypeStruct((n * lines, 128), F32),
+            jax.ShapeDtypeStruct((n * lines, 128), F32),
+            jax.ShapeDtypeStruct((n, extra, 128), jnp.int32),
+            jax.ShapeDtypeStruct((272, tiles), BF),
+        ),
+        in_specs=[vmem] * 7,
+        out_specs=(vmem,) * 4,
+        scratch_shapes=[
+            pltpu.VMEM((2 * lines + extra, 128), BF),
+            pltpu.VMEM((n, 2 * lines + extra, 128), BF),
+            pltpu.SemaphoreType.DMA((n - 1,)),
+            pltpu.SemaphoreType.DMA((n - 1,)),
+        ],
+        compiler_params=pltpu.CompilerParams(
+            collective_id=0, has_side_effects=True, vmem_limit_bytes=32 * 1024 * 1024
+        ),
+    )(vis, pairs, meta, beams, support, gains, jnp.asarray(row_order()))
 
 
 def on_device(visibilities, tile_pairs, owner_tiles, cell_ids, gains, beams, support):
     owners = lax.axis_size("uv")
     me = lax.axis_index("uv").astype(jnp.int32).reshape(1)
     nblocks, _, rows_each = visibilities.shape[1:]
-    band = GRID // owners
-    bands_each = band // KERN
+    bands_each = GRID // owners // KERN
     lines = 2 * nblocks * rows_each // 128
     meta = jnp.concatenate([owner_tiles[0, :, 0], cell_ids[0]]).reshape(-1, 128)
-    meta = jnp.pad(meta, ((0, 16 - meta.shape[0]), (0, 0)))
-    packed = jnp.concatenate(
-        [
-            visibilities.reshape(lines, 128),
-            tile_pairs.reshape(lines, 128).astype(BF),
-            meta.astype(BF),
-        ],
-        axis=0,
-    )
-    gathered = lax.all_gather(packed, "uv", axis=0, tiled=False)
-    vis = gathered[:, :lines].reshape(owners * lines, 128).astype(F32)
-    pairs = gathered[:, lines : 2 * lines].reshape(owners * lines, 128).astype(F32)
-    notes = gathered[:, 2 * lines : 2 * lines + 2 * nblocks // 128].reshape(owners, 2, nblocks)
-    notes = notes.astype(jnp.int32)
+    noted = meta.shape[0]
+    meta = jnp.pad(meta, ((0, 16 - noted), (0, 0)))
+    vis, pairs, notes, table = gather(
+        owners,
+        visibilities.reshape(lines, 128),
+        tile_pairs.reshape(lines, 128),
+        meta,
+        beams,
+        support,
+        gains[0],
+    )
+    notes = notes[:, :noted].reshape(owners, 2, nblocks)
     cells = notes[:, 1]
     places = (cells % COLS) * COLS + notes[:, 0] * bands_each + cells // COLS
-    table = lookup_rows(beams, support, gains[0])
     return make_image(me, places.reshape(-1), vis, pairs, table, owners)
 
 

time: 78.1 us -> 73.3 us (0.939)
  blocking collectives: 15.6 us -> 0 us
  Pallas kernels: 53.9 us -> 64.5 us
  local copies, waits for them, and re-layouts: 1.41 us -> 7.05 us
  other arithmetic: 6.68 us -> 1.33 us
    all_gather x1 -> x0, blocking collectives: 15.6 us -> none  [on_device(): gathered = lax.all_gather(packed, 'uv', axis=0, tiled=False)]
    pallas_call x0 -> x1, Pallas kernels: none -> 10.6 us  [gather(): pl.pallas_call(functools.partial(gather_kernel, n, lines), out_shape=(jax...]
    unnamed x1 -> x17, local copies, waits for them, and re-layouts: 1 us -> 6.77 us
    convert_element_type x4 -> x0, other arithmetic: 2.42 us -> none  [the longest x1 0.86 us: on_device(): tile_pairs.reshape(lines, 128).astype(BF)]
    concatenate x2 -> x0, other arithmetic: 1.53 us -> none  [the longest x1 0.77 us: on_device(): jnp.concatenate([visibilities.reshape(lines, 128), tile_pairs.reshape(lin...]
    squeeze x2 -> x0, other arithmetic: 1.32 us -> none  [on_device(): meta = jnp.concatenate([owner_tiles[0, :, 0], cell_ids[0]]).reshape(-1, 128)]
where the time goes in v3:
time: 73.3 us; the launch traced here: 72.9 us
  Pallas kernels  64.5 us (88%)
  local copies, waits for them, and re-layouts  7.05 us (10%)
  other arithmetic  1.33 us (2%)
    pallas_call x1, Pallas kernels, make_image(): pl.pallas_call(functools.partial(fused_kernel, band, tile, steps), out_sh...  53.9 us
    pallas_call x1, Pallas kernels, gather(): pl.pallas_call(functools.partial(gather_kernel, n, lines), out_shape=(jax...  10.6 us
    unnamed x17, local copies, waits for them, and re-layouts  6.77 us

profile of v3, /device:TPU:0, one launch (start us, length us, event | category | flops | bytes accessed | tf_op | source)
XLA Modules:
  0.0 72.9 jit_solution(6573160548931464505)
XLA Ops:
  0.0 0.7 %add_bitcast_fusion = s32[1,128]{1,0:T(1,128)S(1)} fusion(s32[64]{0:T(128)} %bitcast.11, s32[64]{0:T(128)} %bitcast.12), kind=kLoop, calls=%fused_computation.12 | loop fusion | flops 128 | bytes 1024 | tf_op jit(solution)/shard_map/reshape | solution.py:350
  0.8 0.8 %copy.11.support_ref = s32[256,8]{1,0:T(8,128)S(1)} copy(s32[256,8]{0,1:T(8,128)} %param.16) | data formatting | bytes 16384 | tf_op args[6]
  1.6 0.0 copy-start.3
  1.6 0.9 %copy-done.3 = f32[256,128]{1,0:T(8,128)S(1)} copy-done((f32[256,128]{1,0:T(8,128)S(1)}, f32[256,128]{1,0:T(8,128)}, u32[]{:S(2)}) %copy-start.3) | copy-done | bytes 131096
  2.5 0.0 copy-start.4
  2.5 0.8 %copy-done.4 = s32[64,2,128]{2,1,0:T(2,128)S(1)} copy-done((s32[64,2,128]{2,1,0:T(2,128)S(1)}, s32[64,2,128]{2,1,0:T(2,128)}, u32[]{:S(2)}) %copy-start.4) | copy-done | bytes 65560
  3.3 0.0 copy-start.5
  3.3 0.8 %copy-done.5 = bf16[1,64,2,128]{3,2,1,0:T(2,128)(2,1)S(1)} copy-done((bf16[1,64,2,128]{3,2,1,0:T(2,128)(2,1)S(1)}, bf16[1,64,2,128]{3,2,1,0:T(2,128)(2,1)}, u32[]{:S(2)}) %copy-start.5) | copy-done | bytes 32792
  4.1 0.0 copy-start.6
  4.1 0.8 %copy-done.6 = bf16[128,128]{1,0:T(8,128)(2,1)S(1)} copy-done((bf16[128,128]{1,0:T(8,128)(2,1)S(1)}, bf16[128,128]{1,0:T(8,128)(2,1)}, u32[]{:S(2)}) %copy-start.6) | copy-done | bytes 32792
  4.8 0.0 copy-start.7
  4.8 0.7 copy-done.7
  5.5 10.6 %shard_map.100 = (f32[512,128]{1,0:T(8,128)S(1)}, f32[512,128]{1,0:T(8,128)S(1)}, s32[4,16,128]{2,1,0:T(8,128)S(1)}, bf16[272,256]{1,0:T(8,128)(2,1)S(1)}) custom-call(bf16[128,128]{1,0:T(8,128)(2,1)S(1)} %bitcast.9, s32[128,128]{1,0:T(8,128)S(1)} %bitcast.8, s32[16,128]{1,0:T(8,128)S(1)} %pad.4.meta_ref, f32[256,128]{1,0:T(8,128)S(1)} %copy-done.3, ...), custom_call_target="tpu_custom_call" | custom-call | tf_op jit(solution)/shard_map/pallas_call | solution.py:322
  16.1 0.0 copy-start
  16.1 0.7 copy-done
  16.8 0.0 copy-start.1
  16.8 0.7 copy-done.1
  17.5 0.0 copy-start.2
  17.5 0.6 copy-done.2
  18.1 0.1 reshape.23
  18.3 0.1 squeeze.16
  18.3 0.1 mul.18
  18.4 0.6 fusion.3.place_ref
  19.0 53.9 %shard_map.101 = f32[1,2,512,2048]{3,2,1,0:T(8,128)} custom-call(s32[256]{0:T(256)} %fusion.3.place_ref, s32[1]{0:T(128)} %bitcast.6.me_ref, f32[512,128]{1,0:T(8,128)} %copy-done, f32[512,128]{1,0:T(8,128)} %copy-done.1, bf16[272,256]{1,0:T(8,128)(2,1)} %copy-done.2, bf16[4096,512]{1,0:T(8,128)(2,1)} %constant.44.clone.class_ref, ...), custom_call_target="tpu_custom_call" | custom-call | tf_op jit(solution)/shard_map/pallas_call | solution.py:214
  (3 shorter events, 0.0 us)
Async XLA Ops:
  1.6 0.9 %copy-start.3 = (f32[256,128]{1,0:T(8,128)S(1)}, f32[256,128]{1,0:T(8,128)}, u32[]{:S(2)}) copy-start(f32[256,128]{1,0:T(8,128)} %beams_ref.1) | copy-start | bytes 393220
  2.5 0.8 %copy-start.4 = (s32[64,2,128]{2,1,0:T(2,128)S(1)}, s32[64,2,128]{2,1,0:T(2,128)}, u32[]{:S(2)}) copy-start(s32[64,2,128]{2,1,0:T(2,128)} %param.11) | copy-start | bytes 196612
  3.3 0.8 %copy-start.5 = (bf16[1,64,2,128]{3,2,1,0:T(2,128)(2,1)S(1)}, bf16[1,64,2,128]{3,2,1,0:T(2,128)(2,1)}, u32[]{:S(2)}) copy-start(bf16[1,64,2,128]{3,2,1,0:T(2,128)(2,1)} %param.10) | copy-start | bytes 98308
  4.1 0.8 %copy-start.6 = (bf16[128,128]{1,0:T(8,128)(2,1)S(1)}, bf16[128,128]{1,0:T(8,128)(2,1)}, u32[]{:S(2)}) copy-start(bf16[128,128]{1,0:T(8,128)(2,1)} %constant.43.clone.order_ref) | copy-start | bytes 98308
  4.8 0.7 copy-start.7
  16.1 0.7 copy-start
  16.8 0.7 copy-start.1
  17.5 0.7 copy-start.2

commit v4 on v3

--- a/solution.py
+++ b/solution.py
@@ -318,17 +318,23 @@
     lines = vis.shape[0]
     extra = meta.shape[0]
     tiles = beams.shape[0]
-    vmem = pl.BlockSpec(memory_space=pltpu.VMEM)
+    operands = (vis, pairs, meta, beams, support, gains, jnp.asarray(row_order()))
     return pl.pallas_call(
         functools.partial(gather_kernel, n, lines),
+        grid=(1,),
         out_shape=(
             jax.ShapeDtypeStruct((n * lines, 128), F32),
             jax.ShapeDtypeStruct((n * lines, 128), F32),
             jax.ShapeDtypeStruct((n, extra, 128), jnp.int32),
             jax.ShapeDtypeStruct((272, tiles), BF),
         ),
-        in_specs=[vmem] * 7,
-        out_specs=(vmem,) * 4,
+        in_specs=[pl.BlockSpec(x.shape, lambda i: (0, 0)) for x in operands],
+        out_specs=(
+            pl.BlockSpec((n * lines, 128), lambda i: (0, 0)),
+            pl.BlockSpec((n * lines, 128), lambda i: (0, 0)),
+            pl.BlockSpec((n, extra, 128), lambda i: (0, 0, 0)),
+            pl.BlockSpec((272, tiles), lambda i: (0, 0)),
+        ),
         scratch_shapes=[
             pltpu.VMEM((2 * lines + extra, 128), BF),
             pltpu.VMEM((n, 2 * lines + extra, 128), BF),
@@ -338,7 +344,7 @@
         compiler_params=pltpu.CompilerParams(
             collective_id=0, has_side_effects=True, vmem_limit_bytes=32 * 1024 * 1024
         ),
-    )(vis, pairs, meta, beams, support, gains, jnp.asarray(row_order()))
+    )(*operands)
 
 
 def on_device(visibilities, tile_pairs, owner_tiles, cell_ids, gains, beams, support):

time: 73.3 us -> 73.3 us (level)
  no operation moved by 1% of the time
where the time goes in v4:
time: 73.3 us; the launch traced here: 72.9 us
  Pallas kernels  64.5 us (88%)
  local copies, waits for them, and re-layouts  7.05 us (10%)
  other arithmetic  1.33 us (2%)
    pallas_call x1, Pallas kernels, make_image(): pl.pallas_call(functools.partial(fused_kernel, band, tile, steps), out_sh...  53.9 us
    pallas_call x1, Pallas kernels, gather(): pl.pallas_call(functools.partial(gather_kernel, n, lines), grid=(1,), out...  10.6 us
    unnamed x17, local copies, waits for them, and re-layouts  6.77 us

profile of v4, /device:TPU:0, one launch (start us, length us, event | category | flops | bytes accessed | tf_op | source)
XLA Modules:
  0.0 72.9 jit_solution(6573160548931464505)
XLA Ops:
  0.0 0.7 %add_bitcast_fusion = s32[1,128]{1,0:T(1,128)S(1)} fusion(s32[64]{0:T(128)} %bitcast.11, s32[64]{0:T(128)} %bitcast.12), kind=kLoop, calls=%fused_computation.12 | loop fusion | flops 128 | bytes 1024 | tf_op jit(solution)/shard_map/reshape | solution.py:356
  0.8 0.8 %copy.11.support_ref = s32[256,8]{1,0:T(8,128)S(1)} copy(s32[256,8]{0,1:T(8,128)} %param.16) | data formatting | bytes 16384 | tf_op args[6]
  1.6 0.0 copy-start.3
  1.6 0.9 %copy-done.3 = f32[256,128]{1,0:T(8,128)S(1)} copy-done((f32[256,128]{1,0:T(8,128)S(1)}, f32[256,128]{1,0:T(8,128)}, u32[]{:S(2)}) %copy-start.3) | copy-done | bytes 131096
  2.5 0.0 copy-start.4
  2.5 0.8 %copy-done.4 = s32[64,2,128]{2,1,0:T(2,128)S(1)} copy-done((s32[64,2,128]{2,1,0:T(2,128)S(1)}, s32[64,2,128]{2,1,0:T(2,128)}, u32[]{:S(2)}) %copy-start.4) | copy-done | bytes 65560
  3.3 0.0 copy-start.5
  3.3 0.8 %copy-done.5 = bf16[1,64,2,128]{3,2,1,0:T(2,128)(2,1)S(1)} copy-done((bf16[1,64,2,128]{3,2,1,0:T(2,128)(2,1)S(1)}, bf16[1,64,2,128]{3,2,1,0:T(2,128)(2,1)}, u32[]{:S(2)}) %copy-start.5) | copy-done | bytes 32792
  4.1 0.0 copy-start.6
  4.1 0.8 %copy-done.6 = bf16[128,128]{1,0:T(8,128)(2,1)S(1)} copy-done((bf16[128,128]{1,0:T(8,128)(2,1)S(1)}, bf16[128,128]{1,0:T(8,128)(2,1)}, u32[]{:S(2)}) %copy-start.6) | copy-done | bytes 32792
  4.8 0.0 copy-start.7
  4.8 0.7 copy-done.7
  5.5 10.6 %shard_map.100 = (f32[512,128]{1,0:T(8,128)S(1)}, f32[512,128]{1,0:T(8,128)S(1)}, s32[4,16,128]{2,1,0:T(8,128)S(1)}, bf16[272,256]{1,0:T(8,128)(2,1)S(1)}) custom-call(bf16[128,128]{1,0:T(8,128)(2,1)S(1)} %bitcast.9, s32[128,128]{1,0:T(8,128)S(1)} %bitcast.8, s32[16,128]{1,0:T(8,128)S(1)} %pad.4.meta_ref, f32[256,128]{1,0:T(8,128)S(1)} %copy-done.3, ...), custom_call_target="tpu_custom_call" | custom-call | tf_op jit(solution)/shard_map/pallas_call | solution.py:322
  16.1 0.0 copy-start
  16.1 0.7 copy-done
  16.8 0.0 copy-start.1
  16.8 0.7 copy-done.1
  17.5 0.0 copy-start.2
  17.5 0.6 copy-done.2
  18.1 0.1 reshape.23
  18.3 0.1 squeeze.16
  18.3 0.1 mul.18
  18.4 0.6 fusion.3.place_ref
  19.0 53.9 %shard_map.101 = f32[1,2,512,2048]{3,2,1,0:T(8,128)} custom-call(s32[256]{0:T(256)} %fusion.3.place_ref, s32[1]{0:T(128)} %bitcast.6.me_ref, f32[512,128]{1,0:T(8,128)} %copy-done, f32[512,128]{1,0:T(8,128)} %copy-done.1, bf16[272,256]{1,0:T(8,128)(2,1)} %copy-done.2, bf16[4096,512]{1,0:T(8,128)(2,1)} %constant.44.clone.class_ref, ...), custom_call_target="tpu_custom_call" | custom-call | tf_op jit(solution)/shard_map/pallas_call | solution.py:214
  (3 shorter events, 0.0 us)
Async XLA Ops:
  1.6 0.9 %copy-start.3 = (f32[256,128]{1,0:T(8,128)S(1)}, f32[256,128]{1,0:T(8,128)}, u32[]{:S(2)}) copy-start(f32[256,128]{1,0:T(8,128)} %beams_ref.1) | copy-start | bytes 393220
  2.5 0.8 %copy-start.4 = (s32[64,2,128]{2,1,0:T(2,128)S(1)}, s32[64,2,128]{2,1,0:T(2,128)}, u32[]{:S(2)}) copy-start(s32[64,2,128]{2,1,0:T(2,128)} %param.11) | copy-start | bytes 196612
  3.3 0.8 %copy-start.5 = (bf16[1,64,2,128]{3,2,1,0:T(2,128)(2,1)S(1)}, bf16[1,64,2,128]{3,2,1,0:T(2,128)(2,1)}, u32[]{:S(2)}) copy-start(bf16[1,64,2,128]{3,2,1,0:T(2,128)(2,1)} %param.10) | copy-start | bytes 98308
  4.1 0.8 %copy-start.6 = (bf16[128,128]{1,0:T(8,128)(2,1)S(1)}, bf16[128,128]{1,0:T(8,128)(2,1)}, u32[]{:S(2)}) copy-start(bf16[128,128]{1,0:T(8,128)(2,1)} %constant.43.clone.order_ref) | copy-start | bytes 98308
  4.8 0.7 copy-start.7
  16.1 0.7 copy-start
  16.8 0.7 copy-start.1
  17.5 0.7 copy-start.2
